TPU v7x, 32 devices: a whole 2x2x4 slice. The times are simulated.
32 devices in a mesh: dom: 32 (over z, y, x, core).
Axes of the slice: x: 2, y: 2, z: 4, core: 2. Of those that a mesh axis runs over, the one named last changes fastest.
Arguments:
- particles: float32 [32, 2, 256, 128], P('dom'), may hold values from -60 to 60
- offspring: int32 [32], P('dom'), may hold values from 0 to 7, as said below
- noise: float32 [2, 32, 2, 256, 128], P(None, 'dom'), may hold values from -6 to 6
- accept: int32 [2, 32], P(None, 'dom'), may hold values 0 or 1
- observed: float32 [256, 256], replicated, may hold values from -6 to 6
Outputs:
- moved: float32 [32, 2, 256, 128], P('dom')
- misfit: float32 [2, 32], P(None, 'dom')
Inputs may be any that keep to these rules, and one draw needn't show every extreme that they name: `offspring`: the counts sum to 32. Slot s, numbered by the counts' running sum, is filled by a particle at most 3 places from s, and in every draw some slot is filled from exactly 3 places away.
All inputs are finite; a program needn't handle non-finite values. No bound on the sum of `accept` on one device may be relied on, other than what follows from the above.
Results may differ from a plain program's by a relative error of at most 0.0001.
Values sent between devices are 32-bit elements; how exact they have to be, the bound alone decides.
A program may use at most 64 MiB of HBM per device.

v0:
```python
import functools
import math

import jax
import jax.numpy as jnp
import ml_dtypes
import numpy as np
from jax import lax
from jax.experimental import pallas as pl
from jax.experimental.pallas import tpu as pltpu
from jax.sharding import PartitionSpec as P

REACH = 3
LOW = 16
LANES = 128
COUNT_LANE = 64
PARTS = 2
GROUP_BITS = 3
TEAM = 4
CHUNKS = 8
PIECES = 4

time_step = 0.05
viscosity = 0.001
noise_level = 0.5
spectral_scale = 64.0
prior_amplitude = 1.5
step_size = 0.4

MESH = pl.DeviceIdType.MESH
HBM = pltpu.MemorySpace.HBM


def split_bits(devices):
    bits = devices.bit_length() - 1
    assert 1 << bits == devices
    groups = []
    first = 0
    while first < bits:
        width = min(GROUP_BITS, bits - first)
        groups.append((first, width))
        first += width
    return groups


def filter_kernel(
    devices, groups, x_ref, count_ref, accept_ref, noise_hbm, observed_hbm, *rest
):
    tables_hbm = rest[:6]
    moved_ref, misfit_ref = rest[6:8]
    cand, chosen, sums, small, moved_stage, noise_ref, observed_ref = rest[8:15]
    tables = rest[15:21]
    load_sem, whole_sem, cross_sem, relay_sem, chosen_sem, small_send, small_recv, fetch_sem = rest[21:]
    chunks, chunk_rows, _ = x_ref.shape
    grid = chunks * chunk_rows // PARTS
    me = lax.axis_index("dom")
    place = lax.rem(me, TEAM)
    start = me - place
    core = lax.rem(place, 2)
    side = place // 2
    near = place + 1 - 2 * core
    across = lax.rem(place + 2, TEAM)
    both = lax.rem(near + 2, TEAM)
    sibling, partner = start + near, start + across
    chosen_to = me + TEAM - 2 * TEAM * side
    chosen_from = me - TEAM + 2 * TEAM * side
    sends_chosen = jnp.logical_and(chosen_to >= 0, chosen_to < devices)
    takes_chosen = jnp.logical_and(chosen_from >= 0, chosen_from < devices)
    far_to = jnp.where(place == 0, me - REACH, me + REACH)
    far_from = jnp.where(place == 1, me + REACH, me - REACH)
    outer = jnp.logical_or(place == 0, place == TEAM - 1)
    sends_far = jnp.logical_and(outer, jnp.logical_and(far_to >= 0, far_to < devices))
    takes_far = jnp.logical_and(
        jnp.logical_not(outer), jnp.logical_and(far_from >= 0, far_from < devices)
    )

    load = pltpu.make_async_copy(x_ref, cand.at[place], load_sem)
    load.start()
    fetches = [
        pltpu.make_async_copy(source, target, fetch_sem.at[at])
        for at, (source, target) in enumerate(
            zip((noise_hbm, observed_hbm) + tables_hbm, (noise_ref, observed_ref) + tables)
        )
    ]
    for fetch in fetches:
        fetch.start()

    barrier = pltpu.get_barrier_semaphore()

    def greet(device):
        pl.semaphore_signal(barrier, inc=1, device_id=(device,), device_id_type=MESH)

    partners = []
    for first, width in groups:
        partners.append([jnp.bitwise_xor(me, k << first) for k in range(1, 1 << width)])
    for group in partners:
        for device in group:
            greet(device)
    pl.when(takes_chosen)(lambda: greet(chosen_from))
    pl.when(takes_far)(lambda: greet(far_from))

    load.wait()
    count = count_ref[0].astype(jnp.float32)
    half_low = LOW // 2
    per_part = chunks // PARTS
    blocks = []
    for part in range(PARTS):
        blocks.append(cand[place, part * per_part, :half_low, :])
        blocks.append(cand[place, (part + 1) * per_part - 1, chunk_rows - half_low :, :])
    lane_ids = lax.broadcasted_iota(jnp.int32, (half_low, LANES), 1)
    row_ids = lax.broadcasted_iota(jnp.int32, (half_low, LANES), 0)
    counted = lane_ids >= COUNT_LANE
    order = jnp.where(counted, row_ids * (LANES - COUNT_LANE) + lane_ids - COUNT_LANE, devices)
    package = jnp.where(order == me, count, 0.0)
    for at, block in enumerate(blocks):
        value = block * block * count
        value = value if at == 0 else pltpu.roll(value, at * LOW, 1)
        inside = jnp.logical_and(lane_ids >= at * LOW, lane_ids < (at + 1) * LOW)
        package = jnp.where(inside, value, package)
    sums[0] = package

    expected = sum(len(group) for group in partners)
    pl.semaphore_wait(barrier, expected + sends_chosen.astype(jnp.int32) + sends_far.astype(jnp.int32))

    def remote(source, target, pair, device):
        return pltpu.make_async_remote_copy(
            src_ref=source,
            dst_ref=target,
            send_sem=pair.at[0],
            recv_sem=pair.at[1],
            device_id=(device,),
            device_id_type=MESH,
        )

    def stage_copies(stage):
        copies = []
        base = sum(len(group) for group in partners[:stage])
        for at, device in enumerate(partners[stage]):
            copies.append(
                pltpu.make_async_remote_copy(
                    src_ref=sums.at[stage],
                    dst_ref=small.at[base + at],
                    send_sem=small_send.at[base + at],
                    recv_sem=small_recv.at[base + at],
                    device_id=(device,),
                    device_id_type=MESH,
                )
            )
        return copies

    def cross(slot, chunk):
        return remote(cand.at[slot, chunk], cand.at[slot, chunk], cross_sem.at[chunk], partner)

    def relay(slot, chunk):
        return remote(cand.at[slot, chunk], cand.at[slot, chunk], relay_sem.at[chunk], sibling)

    def forward(chunk):
        return remote(chosen.at[chunk], cand.at[TEAM, chunk], chosen_sem.at[chunk], chosen_to)

    to_sibling = remote(cand.at[place], cand.at[place], whole_sem.at[0], sibling)
    from_sibling = remote(cand.at[near], cand.at[near], whole_sem.at[0], sibling)
    to_far = remote(cand.at[place], cand.at[TEAM + 1], whole_sem.at[1], far_to)

    first_stage = stage_copies(0)
    for copy in first_stage:
        copy.start()
    for chunk in range(chunks):
        cross(place, chunk).start()
    to_sibling.start()
    pl.when(sends_far)(to_far.start)

    def pass_on(chunk):
        cross(across, chunk).wait_recv()
        relay(across, chunk).start()

    stages = [first_stage]
    for stage in range(len(groups)):
        if stage > 0:
            stages.append(stage_copies(stage))
            for copy in stages[stage]:
                copy.start()
        if stage == len(groups) - 1:
            pass_on(0)
        base = sum(len(group) for group in partners[:stage])
        total = sums[stage]
        for at, copy in enumerate(stages[stage]):
            copy.wait_recv()
            total = total + small[base + at]
        sums[stage + 1] = total

    reduced = sums[len(groups)]
    counts = jnp.where(counted, reduced, 0.0)

    def source_place(slot):
        found = jnp.full((1, 1), 1.0, jnp.float32) * (slot - REACH - start).astype(jnp.float32)
        for distance in range(-REACH, REACH):
            ends = jnp.sum(jnp.where(order <= slot + distance, counts, 0.0), keepdims=True)
            found = found + jnp.where(ends <= slot.astype(jnp.float32), 1.0, 0.0)
        return jnp.broadcast_to(found, (chunk_rows, LANES))

    forward_place = source_place(chosen_to)
    from_sibling.wait_recv()

    def team_value(which, chunk):
        value = cand[0, chunk]
        for at in range(1, TEAM):
            value = jnp.where(which == at, cand[at, chunk], value)
        return value

    def send_chosen(chunk):
        relay(both, chunk).wait_recv()
        chosen[chunk] = team_value(forward_place, chunk)
        pl.when(sends_chosen)(forward(chunk).start)

    for chunk in range(1, chunks):
        pass_on(chunk)
        send_chosen(chunk - 1)
    send_chosen(chunks - 1)

    for fetch in fetches:
        fetch.wait()
    work = Work(devices, grid, tables)
    totals = [reduced if at == 0 else pltpu.roll(reduced, LANES - at * LOW, 1) for at in range(2 * PARTS)]
    drift = work.drifts(noise_ref, totals)
    taken = [accept_ref[0, move] == 1 for move in range(len(drift))]
    gains, offsets = work.unrolled(drift, taken)
    offset_states = [work.folded(value) for value in offsets]
    offset_fields = [work.fields(state) for state in offset_states]

    own_place = source_place(me)
    first_side = jnp.broadcast_to(jnp.full((1, 1), 1.0, jnp.float32) * side.astype(jnp.float32), (chunk_rows, LANES)) < 0.5
    before, after = own_place < 0.0, own_place > TEAM - 1.0
    use_chosen = jnp.logical_or(jnp.logical_and(first_side, before), jnp.logical_and(jnp.logical_not(first_side), after))
    use_far = jnp.logical_and(jnp.logical_or(before, after), jnp.logical_not(use_chosen))

    def arrived_far():
        remote(cand.at[TEAM + 1], cand.at[TEAM + 1], whole_sem.at[1], far_from).wait_recv()

    pl.when(takes_far)(arrived_far)
    pieces = []
    for chunk in range(chunks):
        def arrived():
            remote(chosen.at[chunk], cand.at[TEAM, chunk], chosen_sem.at[chunk], chosen_from).wait_recv()

        pl.when(takes_chosen)(arrived)
        value = team_value(own_place, chunk)
        value = jnp.where(use_chosen, cand[TEAM, chunk], value)
        pieces.append(jnp.where(use_far, cand[TEAM + 1, chunk], value))
    present = [jnp.concatenate(pieces[part * per_part : (part + 1) * per_part], axis=0) for part in range(PARTS)]

    moved = present
    for move in range(len(drift)):
        candidate = [work.keep * moved[part] + drift[move][part] for part in range(PARTS)]
        moved = [jnp.where(taken[move], candidate[part], moved[part]) for part in range(PARTS)]
    for part in range(PARTS):
        moved_stage[0, part] = moved[part]
    leave = pltpu.make_async_copy(moved_stage, moved_ref, load_sem)
    leave.start()

    base_state = work.folded(present)
    base_fields = work.fields(base_state)
    states = [gain * base_state + state for gain, state in zip(gains, offset_states)]
    fields = [gain * base_fields + value for gain, value in zip(gains, offset_fields)]
    for move, score in enumerate(work.scores(states, fields, observed_ref)):
        misfit_ref[0, move] = score

    leave.wait()
    for copies in stages:
        for copy in copies:
            copy.wait_send()
    to_sibling.wait_send()
    pl.when(sends_far)(to_far.wait_send)
    for chunk in range(chunks):
        cross(place, chunk).wait_send()
        relay(across, chunk).wait_send()
        pl.when(sends_chosen)(forward(chunk).wait_send)


def halves(table):
    table = np.asarray(table, np.float64)
    high = table.astype(np.float32).astype(ml_dtypes.bfloat16)
    rest = (table - high.astype(np.float64)).astype(np.float32).astype(ml_dtypes.bfloat16)
    return np.stack([high, rest])


def make_tables(grid):
    half = grid // 2
    angle = 2.0 * math.pi / grid
    index = np.arange(grid)
    low = np.arange(half)
    phase = (index[:, None] * low[None, :] % grid) * angle
    sines = np.sin(phase)
    sines[:, 0] = 1.0 - 2.0 * (index % 2)
    fold = np.concatenate([np.cos(phase), sines], axis=1)
    weight = np.where(low == 0, 1.0, 2.0)[:, None]
    back = np.concatenate([weight * np.cos(phase).T, -weight * np.sin(phase).T], axis=0) / spectral_scale
    fore = np.concatenate([np.cos(phase), -np.sin(phase)], axis=1) * (spectral_scale / (grid * grid))
    flip = np.zeros((half, half))
    flip[low, (half - low) % half] = 1.0
    wave_y = np.concatenate([low, np.where(low == 0, half, low)]).astype(np.float64)[:, None]
    wave_x = low.astype(np.float64)[None, :]
    square = wave_y**2 + wave_x**2
    inverse = np.where(square > 0, 1.0 / np.maximum(square, 1.0), 0.0)
    damping = 1.0 / (1.0 + time_step * viscosity * square)
    keeper = (np.abs(wave_y) <= grid // 3) & (wave_x <= grid // 3)
    doubled = np.where(np.concatenate([low, low])[:, None] == 0, 1.0, 2.0)
    flux = -time_step * keeper * doubled * damping
    signed = np.where(index < half, index, index - grid).astype(np.float64)[:, None]
    prior = prior_amplitude / (1.0 + np.sqrt(signed**2 + wave_x**2) / 8.0)
    scales = np.stack([inverse, damping, flux, step_size * prior]).astype(np.float32)
    return (
        halves(fold), halves(fold.T), halves(back), halves(fore),
        flip.astype(ml_dtypes.bfloat16), scales,
    )


def split(value):
    high = value.astype(jnp.bfloat16)
    return high, (value - high.astype(jnp.float32)).astype(jnp.bfloat16)


def dot(a, b):
    return jnp.dot(a, b, preferred_element_type=jnp.float32)


def table_left(table, value):
    high, rest = split(value)
    return dot(table[0], high) + dot(table[0], rest) + dot(table[1], high)


def table_right(value, table):
    high, rest = split(value)
    return dot(high, table[0]) + dot(rest, table[0]) + dot(high, table[1])


class Work:
    def __init__(self, devices, grid, tables):
        fold, unfold, back, fore, flip, scales = tables
        self.devices, self.grid, self.half = devices, grid, grid // 2
        self.fold = (fold[0], fold[1])
        self.unfold = (unfold[0], unfold[1])
        self.back = (back[0], back[1])
        self.fore = (fore[0], fore[1])
        self.flip = flip[...]
        self.scales = scales
        self.keep = math.sqrt(1.0 - step_size * step_size)
        row_ids = lax.broadcasted_iota(jnp.int32, (self.half, grid), 0)
        self.first = row_ids == 0
        self.wave = row_ids.astype(jnp.float32)
        self.wave_x = lax.broadcasted_iota(jnp.int32, (grid, self.half), 1).astype(jnp.float32)

    def wide(self, index):
        value = self.scales[index]
        return jnp.concatenate([value, value], axis=1)

    def turn(self, value):
        return jnp.concatenate([-value[:, self.half :], value[:, : self.half]], axis=1)

    def drifts(self, noise_ref, totals):
        half_low = LOW // 2
        lanes = lax.broadcasted_iota(jnp.int32, (half_low, self.half), 1)
        prior = self.scales[3]
        inner = slice(half_low, self.grid - half_low)
        spreads = []
        for part in range(PARTS):
            head, tail = [
                step_size * jnp.sqrt(total * (1.0 / self.devices) + 1e-06)
                for total in totals[2 * part : 2 * part + 2]
            ]
            top = jnp.where(lanes < LOW, head, prior[:half_low])
            bottom = jnp.where(lanes < LOW, tail, prior[self.grid - half_low :])
            spreads.append(jnp.concatenate([top, prior[inner], bottom], axis=0))
        return [
            [spreads[part] * noise_ref[move, 0, part] for part in range(PARTS)]
            for move in range(noise_ref.shape[0])
        ]

    def unrolled(self, drift, taken):
        gain, offset = 1.0, [jnp.zeros_like(value) for value in drift[0]]
        gains, offsets = [], []
        for step, accepted in zip(drift, taken):
            new_gain = self.keep * gain
            new_offset = [self.keep * old + value for old, value in zip(offset, step)]
            gains.append(new_gain)
            offsets.append(new_offset)
            gain = jnp.where(accepted, new_gain, gain)
            offset = [jnp.where(accepted, new, old) for new, old in zip(new_offset, offset)]
        return gains, offsets

    def folded(self, parts):
        half = self.half
        top = jnp.concatenate([part[:half] for part in parts], axis=1)
        high, rest = split(jnp.concatenate([part[half:] for part in parts], axis=1))
        other = dot(self.flip, high) + dot(self.flip, rest)
        even = top + jnp.where(self.first, 0.0, other)
        odd = jnp.where(self.first, other, self.turn(top - other))
        return jnp.concatenate([even, odd], axis=0)

    def fields(self, state):
        half, wave_x = self.half, self.wave_x
        psi = state * self.wide(0)
        even, odd = psi[:half], psi[half:]
        along_y = jnp.concatenate(
            [self.wave * odd, jnp.where(self.first, -float(half) * self.turn(odd), -self.wave * even)], axis=0
        )
        along_x = jnp.concatenate([wave_x * psi[:, half:], -wave_x * psi[:, :half]], axis=1)
        rows = [table_left(self.fold, value) for value in (state, along_y, along_x)]
        return table_right(jnp.concatenate(rows, axis=0), self.back)

    def scores(self, states, fields, observed_ref):
        grid, half, wave, wave_x = self.grid, self.half, self.wave, self.wave_x
        products = []
        for value in fields:
            vort = value[:grid]
            products += [value[grid : 2 * grid] * vort, value[2 * grid :] * vort]
        rows = table_right(jnp.concatenate(products, axis=0), self.fore)
        damping, flux_scale = self.wide(1), self.wide(2)
        finals = []
        for move, state in enumerate(states):
            flux_u = table_left(self.unfold, rows[(2 * move) * grid : (2 * move + 1) * grid])
            flux_v = table_left(self.unfold, rows[(2 * move + 1) * grid : (2 * move + 2) * grid])
            along_x = jnp.concatenate([-wave_x * flux_u[:, half:], wave_x * flux_u[:, :half]], axis=1)
            along_y = jnp.concatenate([wave * flux_v[half:], -wave * flux_v[:half]], axis=0)
            finals.append(table_left(self.fold, state * damping + flux_scale * (along_x + along_y)))
        forecast = table_right(jnp.concatenate(finals, axis=0), self.back)
        scale = 1.0 / (2.0 * noise_level * noise_level * grid * grid)
        result = []
        for move in range(len(states)):
            gap = forecast[move * grid : (move + 1) * grid] - observed_ref[...]
            result.append(jnp.sum(gap * gap) * scale)
        return result


def settle_kernel(moved_ref, misfit_ref, moved_out, misfit_out, stage, sems):
    pieces = sems.shape[1]
    parts, rows = moved_ref.shape[1], moved_ref.shape[2]
    span = parts * rows // pieces
    per_part = pieces // parts
    reads, writes = [], []
    for at in range(pieces):
        where = (0, at // per_part, pl.ds(at % per_part * span, span))
        reads.append(pltpu.make_async_copy(moved_ref.at[where], stage.at[at], sems.at[0, at]))
        writes.append(pltpu.make_async_copy(stage.at[at], moved_out.at[where], sems.at[1, at]))
    for copy in reads:
        copy.start()
    for move in range(misfit_ref.shape[1]):
        misfit_out[0, move] = misfit_ref[0, move]
    for read, write in zip(reads, writes):
        read.wait()
        write.start()
    for copy in writes:
        copy.wait()


def settle(moved, misfit):
    hbm = pl.BlockSpec(memory_space=HBM)
    smem = pl.BlockSpec(memory_space=pltpu.SMEM)
    return pl.pallas_call(
        settle_kernel,
        out_shape=tuple(jax.ShapeDtypeStruct(value.shape, value.dtype) for value in (moved, misfit)),
        in_specs=[hbm, smem],
        out_specs=(hbm, smem),
        scratch_shapes=[
            pltpu.VMEM((PIECES, moved.shape[1] * moved.shape[2] // PIECES, moved.shape[3]), moved.dtype),
            pltpu.SemaphoreType.DMA((2, PIECES)),
        ],
        compiler_params=pltpu.CompilerParams(vmem_limit_bytes=63 * 1024 * 1024),
        name="settle",
    )(moved, misfit)


def body(devices, particles, offspring, noise, accept, observed):
    groups = split_bits(devices)
    _, _, grid, half = particles.shape
    moves = noise.shape[0]
    assert particles.shape[0] == 1 and half == LANES and devices <= LOW // 2 * (LANES - COUNT_LANE)
    copies = sum((1 << width) - 1 for _, width in groups)
    package = LOW // 2
    assert 2 * PARTS * LOW == COUNT_LANE
    slots = TEAM + 2
    assert devices % TEAM == 0 and (PARTS * grid) % CHUNKS == 0
    chunk_shape = (CHUNKS, PARTS * grid // CHUNKS, half)
    tables = [jnp.asarray(table) for table in make_tables(grid)]
    hbm = pl.BlockSpec(memory_space=HBM)
    smem = pl.BlockSpec(memory_space=pltpu.SMEM)
    fetched = [noise, observed] + tables
    moved, misfit = pl.pallas_call(
        functools.partial(filter_kernel, devices, groups),
        out_shape=(
            jax.ShapeDtypeStruct((1, PARTS, grid, half), jnp.float32),
            jax.ShapeDtypeStruct((1, moves), jnp.float32),
        ),
        in_specs=[hbm, smem, smem] + [hbm] * len(fetched),
        out_specs=(hbm, smem),
        scratch_shapes=[
            pltpu.VMEM((slots,) + chunk_shape, jnp.float32),
            pltpu.VMEM(chunk_shape, jnp.float32),
            pltpu.VMEM((len(groups) + 1, package, LANES), jnp.float32),
            pltpu.VMEM((copies, package, LANES), jnp.float32),
            pltpu.VMEM((1, PARTS, grid, half), jnp.float32),
        ]
        + [pltpu.VMEM(value.shape, value.dtype) for value in fetched]
        + [
            pltpu.SemaphoreType.DMA,
            pltpu.SemaphoreType.DMA((2, 2)),
            pltpu.SemaphoreType.DMA((CHUNKS, 2)),
            pltpu.SemaphoreType.DMA((CHUNKS, 2)),
            pltpu.SemaphoreType.DMA((CHUNKS, 2)),
            pltpu.SemaphoreType.DMA((copies,)),
            pltpu.SemaphoreType.DMA((copies,)),
            pltpu.SemaphoreType.DMA((len(fetched),)),
        ],
        compiler_params=pltpu.CompilerParams(
            collective_id=0, has_side_effects=True, vmem_limit_bytes=63 * 1024 * 1024
        ),
        name="filter",
    )(particles.reshape(chunk_shape), offspring, accept.T, *fetched)
    moved, misfit = settle(moved, misfit)
    return moved, misfit.T


def solution(mesh):
    return jax.shard_map(
        functools.partial(body, mesh.shape["dom"]),
        mesh=mesh,
        in_specs=(
            P("dom", None, None, None),
            P("dom"),
            P(None, "dom", None, None, None),
            P(None, "dom"),
            P(),
        ),
        out_specs=(P("dom", None, None, None), P(None, "dom")),
        check_vma=False,
    )
```

profile of v0, /device:TPU:7, one launch (start us, length us, event | category | flops | bytes accessed | tf_op | source)
XLA Modules:
  0.0 30.5 jit_solution(4887179964187321263)
XLA Ops:
  1.3 26.4 %filter.1 = (f32[1,2,256,128]{3,2,1,0:T(8,128)}, f32[1,2]{1,0:T(1,128)}) custom-call(f32[8,64,128]{2,1,0:T(8,128)} %bitcast.3, s32[1]{0:T(128)S(6)} %copy.13.count_ref, s32[1,2]{1,0:T(1,128)} %bitcast.4, f32[2,1,2,256,128]{4,3,2,1,0:T(8,128)} %noise_hbm.1, f32[256,256]{1,0:T(8,128)} %observed_hbm.1, bf16[2,256,256]{2,1,0:T(8,128)(2,1)} %constant.12.clone.rest_0_, ...), custom_call_target="tpu_custom_call" | custom-call | tf_op jit(solution)/shard_map/filter/pallas_call | solution.py:487
  27.7 2.8 %settle.1 = (f32[1,2,256,128]{3,2,1,0:T(8,128)}, f32[1,2]{1,0:T(1,128)}) custom-call(f32[1,2,256,128]{3,2,1,0:T(8,128)} %get-tuple-element.6.moved_ref, f32[1,2]{1,0:T(1,128)} %get-tuple-element.7.misfit_ref), custom_call_target="tpu_custom_call" | custom-call | tf_op jit(solution)/shard_map/settle/pallas_call | solution.py:458
where the time goes:
time: 30.7 us; the launch traced here: 30.5 us
  Pallas kernels  29.2 us (95%)
  between operations  1.28 us (4%)
    pallas_call x1, Pallas kernels, body(): pl.pallas_call(functools.partial(filter_kernel, devices, groups), out_sha...  26.4 us
    pallas_call x1, Pallas kernels, settle(): pl.pallas_call(settle_kernel, out_shape=tuple((jax.ShapeDtypeStruct(value...  2.81 us

commit v1 on v0

--- a/solution.py
+++ b/solution.py
@@ -17,8 +17,7 @@
 PARTS = 2
 GROUP_BITS = 3
 TEAM = 4
-CHUNKS = 8
-PIECES = 4
+CHUNKS = 4
 
 time_step = 0.05
 viscosity = 0.001
@@ -82,9 +81,6 @@
             zip((noise_hbm, observed_hbm) + tables_hbm, (noise_ref, observed_ref) + tables)
         )
     ]
-    for fetch in fetches:
-        fetch.start()
-
     barrier = pltpu.get_barrier_semaphore()
 
     def greet(device):
@@ -168,6 +164,8 @@
         cross(place, chunk).start()
     to_sibling.start()
     pl.when(sends_far)(to_far.start)
+    for fetch in fetches:
+        fetch.start()
 
     def pass_on(chunk):
         cross(across, chunk).wait_recv()
@@ -429,44 +427,6 @@
             gap = forecast[move * grid : (move + 1) * grid] - observed_ref[...]
             result.append(jnp.sum(gap * gap) * scale)
         return result
-
-
-def settle_kernel(moved_ref, misfit_ref, moved_out, misfit_out, stage, sems):
-    pieces = sems.shape[1]
-    parts, rows = moved_ref.shape[1], moved_ref.shape[2]
-    span = parts * rows // pieces
-    per_part = pieces // parts
-    reads, writes = [], []
-    for at in range(pieces):
-        where = (0, at // per_part, pl.ds(at % per_part * span, span))
-        reads.append(pltpu.make_async_copy(moved_ref.at[where], stage.at[at], sems.at[0, at]))
-        writes.append(pltpu.make_async_copy(stage.at[at], moved_out.at[where], sems.at[1, at]))
-    for copy in reads:
-        copy.start()
-    for move in range(misfit_ref.shape[1]):
-        misfit_out[0, move] = misfit_ref[0, move]
-    for read, write in zip(reads, writes):
-        read.wait()
-        write.start()
-    for copy in writes:
-        copy.wait()
-
-
-def settle(moved, misfit):
-    hbm = pl.BlockSpec(memory_space=HBM)
-    smem = pl.BlockSpec(memory_space=pltpu.SMEM)
-    return pl.pallas_call(
-        settle_kernel,
-        out_shape=tuple(jax.ShapeDtypeStruct(value.shape, value.dtype) for value in (moved, misfit)),
-        in_specs=[hbm, smem],
-        out_specs=(hbm, smem),
-        scratch_shapes=[
-            pltpu.VMEM((PIECES, moved.shape[1] * moved.shape[2] // PIECES, moved.shape[3]), moved.dtype),
-            pltpu.SemaphoreType.DMA((2, PIECES)),
-        ],
-        compiler_params=pltpu.CompilerParams(vmem_limit_bytes=63 * 1024 * 1024),
-        name="settle",
-    )(moved, misfit)
 
 
 def body(devices, particles, offspring, noise, accept, observed):
@@ -515,7 +475,6 @@
         ),
         name="filter",
     )(particles.reshape(chunk_shape), offspring, accept.T, *fetched)
-    moved, misfit = settle(moved, misfit)
     return moved, misfit.T
 
 

time: 30.7 us -> 28.8 us (0.938)
  Pallas kernels: 29.2 us -> 25.2 us
  local copies, waits for them, and re-layouts: 0 us -> 2.19 us
    pallas_call x1 -> x0, Pallas kernels: 2.81 us -> none  [settle(): pl.pallas_call(settle_kernel, out_shape=tuple((jax.ShapeDtypeStruct(value...]
    unnamed x0 -> x4, local copies, waits for them, and re-layouts: none -> 2.19 us
    pallas_call x1, Pallas kernels: 26.4 us -> 25.2 us  [body(): pl.pallas_call(functools.partial(filter_kernel, devices, groups), out_sha...]
where the time goes in v1:
time: 28.8 us; the launch traced here: 28.6 us
  Pallas kernels  25.2 us (88%)
  local copies, waits for them, and re-layouts  2.19 us (8%)
  between operations  1.29 us (4%)
    pallas_call x1, Pallas kernels, body(): pl.pallas_call(functools.partial(filter_kernel, devices, groups), out_sha...  25.2 us
    unnamed x4, local copies, waits for them, and re-layouts  2.19 us

profile of v1, /device:TPU:7, one launch (start us, length us, event | category | flops | bytes accessed | tf_op | source)
XLA Modules:
  0.0 28.6 jit_solution(13189161366859356160)
XLA Ops:
  1.3 25.2 %filter.1 = (f32[1,2,256,128]{3,2,1,0:T(8,128)}, f32[1,2]{1,0:T(1,128)}) custom-call(f32[4,128,128]{2,1,0:T(8,128)} %bitcast.3, s32[1]{0:T(128)S(6)} %copy.15.count_ref, s32[1,2]{1,0:T(1,128)} %bitcast.4, f32[2,1,2,256,128]{4,3,2,1,0:T(8,128)} %noise_hbm.1, f32[256,256]{1,0:T(8,128)} %observed_hbm.1, bf16[2,256,256]{2,1,0:T(8,128)(2,1)} %constant.12.clone.rest_0_, ...), custom_call_target="tpu_custom_call" | custom-call | tf_op jit(solution)/shard_map/filter/pallas_call | solution.py:447
  26.4 0.0 copy-start
  26.5 1.7 %copy.16 = f32[1,2,256,128]{3,2,1,0:T(8,128)} copy(f32[1,2,256,128]{3,2,1,0:T(8,128)} %get-tuple-element.8) | data formatting | bytes 524288
  28.1 0.0 copy-done
  28.1 0.5 %copy.17 = f32[2,1]{0,1:T(1,128)} copy(f32[2,1]{0,1:T(1,128)S(1)} %bitcast.5) | data formatting | bytes 16
Async XLA Ops:
  26.4 1.7 %copy-start = (f32[1,2]{1,0:T(1,128)S(1)}, f32[1,2]{1,0:T(1,128)}, u32[]{:S(2)}) copy-start(f32[1,2]{1,0:T(1,128)} %get-tuple-element.5) | copy-start | bytes 28

commit v2 on v1

--- a/solution.py
+++ b/solution.py
@@ -17,7 +17,7 @@
 PARTS = 2
 GROUP_BITS = 3
 TEAM = 4
-CHUNKS = 4
+CHUNKS = 2
 
 time_step = 0.05
 viscosity = 0.001

time: 28.8 us -> 29 us (level)
  the two profiles are of different devices: /device:TPU:7 before, /device:TPU:8 now
where the time goes in v2:
time: 29 us; the launch traced here: 28.8 us
  Pallas kernels  25.3 us (87%)
  local copies, waits for them, and re-layouts  2.19 us (8%)
  between operations  1.29 us (4%)
    pallas_call x1, Pallas kernels, body(): pl.pallas_call(functools.partial(filter_kernel, devices, groups), out_sha...  25.3 us
    unnamed x4, local copies, waits for them, and re-layouts  2.19 us

profile of v2, /device:TPU:8, one launch (start us, length us, event | category | flops | bytes accessed | tf_op | source)
XLA Modules:
  0.0 28.8 jit_solution(10868943174704693621)
XLA Ops:
  1.3 25.3 %filter.1 = (f32[1,2,256,128]{3,2,1,0:T(8,128)}, f32[1,2]{1,0:T(1,128)}) custom-call(f32[2,256,128]{2,1,0:T(8,128)} %bitcast.3, s32[1]{0:T(128)S(6)} %copy.15.count_ref, s32[1,2]{1,0:T(1,128)} %bitcast.4, f32[2,1,2,256,128]{4,3,2,1,0:T(8,128)} %noise_hbm.1, f32[256,256]{1,0:T(8,128)} %observed_hbm.1, bf16[2,256,256]{2,1,0:T(8,128)(2,1)} %constant.12.clone.rest_0_, ...), custom_call_target="tpu_custom_call" | custom-call | tf_op jit(solution)/shard_map/filter/pallas_call | solution.py:447
  26.6 0.0 copy-start
  26.6 1.7 %copy.16 = f32[1,2,256,128]{3,2,1,0:T(8,128)} copy(f32[1,2,256,128]{3,2,1,0:T(8,128)} %get-tuple-element.8) | data formatting | bytes 524288
  28.3 0.0 copy-done
  28.3 0.5 %copy.17 = f32[2,1]{0,1:T(1,128)} copy(f32[2,1]{0,1:T(1,128)S(1)} %bitcast.5) | data formatting | bytes 16
Async XLA Ops:
  26.6 1.7 %copy-start = (f32[1,2]{1,0:T(1,128)S(1)}, f32[1,2]{1,0:T(1,128)}, u32[]{:S(2)}) copy-start(f32[1,2]{1,0:T(1,128)} %get-tuple-element.5) | copy-start | bytes 28
